TPU v7x, 32 devices: a whole 2x2x4 slice. The times are simulated.
32 devices in a mesh: rows: 4 (over z), cols: 2 (over core), heads: 4 (over y, x).
Axes of the slice: x: 2, y: 2, z: 4, core: 2. Of those that a mesh axis runs over, the one named last changes fastest.
Arguments:
- queries: bfloat16 [256, 32, 1280], P(('rows', 'heads'), 'cols'), may hold values from -5 to 5
- key_rows: bfloat16 [256, 32, 1280], P(('rows', 'heads'), 'cols'), may hold values from -5 to 5
- value_rows: bfloat16 [256, 32, 1280], P(('rows', 'heads'), 'cols'), may hold values from -5 to 5
- out_grad: bfloat16 [256, 32, 1280], P(('rows', 'heads'), 'cols'), may hold values from -5 to 5
- pattern: int32 [32, 4], replicated, may hold values from 0 to 511
- tissue: int32 [32, 4], replicated, may hold values 0 or 1
Outputs:
- query_grad: bfloat16 [256, 32, 1280], P(('rows', 'heads'), 'cols')
- key_grad: bfloat16 [256, 32, 1280], P(('rows', 'heads'), 'cols')
- value_grad: bfloat16 [256, 32, 1280], P(('rows', 'heads'), 'cols')
All inputs are finite; a program needn't handle non-finite values.
Results may differ from a plain program's by a relative error of at most 0.0067.
Values may be sent and summed in bfloat16 or wider, within the bound.
A program may use at most 128 MiB of HBM per device.

v0:
```python
import math

import jax
import jax.numpy as jnp
from jax import lax
from jax.sharding import PartitionSpec as P

HDIM = 80
TILE_SIDE = 8


def with_halo(shard, sides, width):
    for axis, dim in sides:
        size, length = (lax.axis_size(axis), shard.shape[dim])
        up = [(i, (i + 1) % size) for i in range(size - 1)]
        down = [(j, i) for i, j in up]
        last = lax.slice_in_dim(shard, length - width, length, axis=dim)
        first = lax.slice_in_dim(shard, 0, width, axis=dim)
        before = lax.ppermute(last, axis, up)
        after = lax.ppermute(first, axis, down)
        shard = jnp.concatenate([before, shard, after], axis=dim)
    return shard


def cell_at(indices):
    return tuple((jnp.asarray(item).astype(jnp.int32) for item in indices))


def product(form, left, right):
    return jnp.einsum(form, left, right, preferred_element_type=jnp.float32)


def neighbour_mask(pattern, tissue_pad, tile_row, first_col, tile_cols):
    pattern_row = lax.dynamic_slice(pattern, cell_at((tile_row, first_col)), (1, tile_cols))[0]
    tissue_near = lax.dynamic_slice(tissue_pad, cell_at((tile_row, first_col)), (3, tile_cols + 2))
    slots = []
    for a in range(3):
        for b in range(3):
            if a == 1 and b == 1:
                slots.append(pattern_row >= 0)
            else:
                bit_set = jnp.right_shift(pattern_row, 3 * a + b) & 1
                slots.append((bit_set == 1) & (tissue_near[a, b : b + tile_cols] == 1))
    return jnp.stack(slots, 1)


def tile_backward(queries, padded, out_grad, pattern, tissue, first_row, first_col, width):
    tile_side = TILE_SIDE
    row_count, col_count, features = queries.shape
    tile_rows = row_count // tile_side
    tile_cols = col_count // tile_side
    group_heads = width // HDIM
    group_count = features // width
    tile_area = tile_side * tile_side
    score_scale = 1.0 / math.sqrt(HDIM)
    tissue_pad = jnp.pad(tissue, 1)

    def to_tiles(block):
        block = block.reshape(tile_side, tile_cols, tile_side, group_heads, HDIM)
        return block.transpose(1, 3, 0, 2, 4).reshape(tile_cols, group_heads, tile_area, HDIM)

    def tile_step(carried, index):
        query_grads, totals = carried
        tile_row = index // group_count
        group_at = index % group_count * width
        row_at = tile_row * tile_side
        query_tile = to_tiles(
            lax.dynamic_slice(
                queries, cell_at((row_at, 0, group_at)), (tile_side, col_count, width)
            )
        )
        grad_tile = to_tiles(
            lax.dynamic_slice(
                out_grad, cell_at((row_at, 0, group_at)), (tile_side, col_count, width)
            )
        )
        key_band = lax.dynamic_slice(
            padded,
            cell_at((row_at, 0, 0, group_at)),
            (3 * tile_side, col_count + 2 * tile_side, 2, width),
        )
        shifted = jnp.stack(
            [key_band[:, b * tile_side : b * tile_side + col_count] for b in range(3)]
        )
        shifted = shifted.reshape(3, 3, tile_side, tile_cols, tile_side, 2, group_heads, HDIM)
        shifted = shifted.transpose(5, 3, 6, 1, 0, 2, 4, 7).reshape(
            2, tile_cols, group_heads, 9 * tile_area, HDIM
        )
        near_keys = shifted[0]
        near_values = shifted[1]
        allowed = neighbour_mask(pattern, tissue_pad, first_row + tile_row, first_col, tile_cols)
        key_mask = jnp.repeat(allowed, tile_area, axis=1)[:, None, None, :]
        scores = product("jhqd,jhkd->jhqk", query_tile, near_keys) * score_scale
        scores = jnp.where(key_mask, scores, -1e30)
        row_max = jnp.max(scores, axis=-1, keepdims=True)
        exp_scores = jnp.exp(scores - row_max)
        weights = exp_scores / jnp.sum(exp_scores, axis=-1, keepdims=True)
        weight_grad = product("jhqd,jhkd->jhqk", grad_tile, near_values)
        row_dot = jnp.sum(weights * weight_grad, axis=-1, keepdims=True)
        score_grad = (weights * (weight_grad - row_dot)).astype(jnp.bfloat16)
        weights_low = weights.astype(jnp.bfloat16)
        query_part = product("jhqk,jhkd->jhqd", score_grad, near_keys) * score_scale
        key_part = product("jhqk,jhqd->jhkd", score_grad, query_tile) * score_scale
        value_part = product("jhqk,jhqd->jhkd", weights_low, grad_tile)
        kv_parts = jnp.stack([key_part, value_part], 0).reshape(
            2, tile_cols, group_heads, 3, 3, tile_side, tile_side, HDIM
        )
        kv_parts = kv_parts.transpose(4, 3, 5, 1, 6, 0, 2, 7).reshape(
            3, 3 * tile_side, col_count, 2, width
        )
        for b in range(3):
            place = cell_at((row_at, b * tile_side, 0, group_at))
            previous = lax.dynamic_slice(totals, place, kv_parts.shape[1:])
            totals = lax.dynamic_update_slice(totals, previous + kv_parts[b], place)
        query_low = query_part.reshape(
            tile_cols, group_heads, tile_side, tile_side, HDIM
        ).transpose(2, 0, 3, 1, 4)
        query_low = query_low.reshape(tile_side, col_count, width).astype(jnp.bfloat16)
        query_grads = lax.dynamic_update_slice(
            query_grads, query_low, cell_at((row_at, 0, group_at))
        )
        return ((query_grads, totals), None)

    start = (
        jnp.zeros(queries.shape, jnp.bfloat16),
        jnp.zeros((row_count + 2 * tile_side, col_count + 2 * tile_side, 2, features), jnp.float32),
    )
    (query_grads, totals), _ = lax.scan(
        tile_step, start, jnp.arange(tile_rows * group_count, dtype=jnp.int32)
    )
    return (query_grads, totals)


def fold_rows(extended, row_count, tile_side):
    middle = extended[2 * tile_side : row_count + 2 * tile_side]
    middle = middle.at[:tile_side].add(extended[:tile_side])
    return middle.at[row_count - tile_side :].add(extended[row_count + 3 * tile_side :])


def shards(queries, key_rows, value_rows, out_grad, pattern, tissue):
    tile_side = TILE_SIDE
    slab_rows, width_dev, model_width = queries.shape
    moved = (
        lax.all_to_all(
            lax.all_to_all(queries, "cols", split_axis=2, concat_axis=1, tiled=True),
            "heads",
            split_axis=2,
            concat_axis=0,
            tiled=True,
        ),
        lax.all_to_all(
            lax.all_to_all(key_rows, "cols", split_axis=2, concat_axis=1, tiled=True),
            "heads",
            split_axis=2,
            concat_axis=0,
            tiled=True,
        ),
        lax.all_to_all(
            lax.all_to_all(value_rows, "cols", split_axis=2, concat_axis=1, tiled=True),
            "heads",
            split_axis=2,
            concat_axis=0,
            tiled=True,
        ),
        lax.all_to_all(
            lax.all_to_all(out_grad, "cols", split_axis=2, concat_axis=1, tiled=True),
            "heads",
            split_axis=2,
            concat_axis=0,
            tiled=True,
        ),
    )
    head_query, head_key, head_value, head_grad = moved
    row_count, col_count, features = head_query.shape
    first_row = lax.axis_index("rows") * (row_count // tile_side)
    stacked = jnp.pad(
        jnp.stack([head_key, head_value], 2), ((0, 0), (tile_side, tile_side), (0, 0), (0, 0))
    )
    padded = with_halo(stacked, (("rows", 0),), tile_side)
    query_grads, totals = tile_backward(
        head_query, padded, head_grad, pattern, tissue, first_row, 0, features
    )
    query_five = query_grads.reshape(row_count, col_count, 1, 1, features)
    extended = with_halo(totals[:, tile_side : col_count + tile_side], (("rows", 0),), tile_side)
    summed = fold_rows(extended, row_count, tile_side).astype(jnp.bfloat16)
    key_five = summed[:, :, 0].reshape(row_count, col_count, 1, 1, features)
    value_five = summed[:, :, 1].reshape(row_count, col_count, 1, 1, features)
    query_back, key_back, value_back = (
        lax.all_to_all(
            lax.all_to_all(query_five, "cols", split_axis=1, concat_axis=2, tiled=True),
            "heads",
            split_axis=0,
            concat_axis=3,
            tiled=True,
        ),
        lax.all_to_all(
            lax.all_to_all(key_five, "cols", split_axis=1, concat_axis=2, tiled=True),
            "heads",
            split_axis=0,
            concat_axis=3,
            tiled=True,
        ),
        lax.all_to_all(
            lax.all_to_all(value_five, "cols", split_axis=1, concat_axis=2, tiled=True),
            "heads",
            split_axis=0,
            concat_axis=3,
            tiled=True,
        ),
    )
    return (
        query_back.reshape(slab_rows, width_dev, model_width),
        key_back.reshape(slab_rows, width_dev, model_width),
        value_back.reshape(slab_rows, width_dev, model_width),
    )


def solution(mesh):
    placed = (
        P(("rows", "heads"), "cols", None),
        P(("rows", "heads"), "cols", None),
        P(("rows", "heads"), "cols", None),
        P(("rows", "heads"), "cols", None),
        P(),
        P(),
    )
    return jax.shard_map(
        shards,
        mesh=mesh,
        in_specs=placed,
        out_specs=(
            P(("rows", "heads"), "cols", None),
            P(("rows", "heads"), "cols", None),
            P(("rows", "heads"), "cols", None),
        ),
        check_vma=False,
    )
```

profile of v0, /device:TPU:21, one launch (start us, length us, event | category | flops | bytes accessed | tf_op | source)
XLA Modules:
  0.0 765.0 jit_solution(12944244360682047668)
XLA Ops:
  0.6 5.8 copy.103
  6.4 7.9 %reshape.554 = bf16[2,2,81920]{2,1,0:T(2,128)(2,1)} reshape(bf16[1280,16,16]{2,1,0:T(8,128)(2,1)} %bitcast.204) | data formatting | bytes 1310720
  18.5 4.6 copy.97
  23.1 7.9 %reshape.546 = bf16[2,2,81920]{2,1,0:T(2,128)(2,1)} reshape(bf16[1280,16,16]{2,1,0:T(8,128)(2,1)} %bitcast.205) | data formatting | bytes 1310720
  31.0 4.7 all-to-all-start
  35.7 5.4 reshape.555
  41.2 6.9 copy.142
  54.8 4.6 copy.109
  59.5 7.2 reshape.550
  66.7 4.6 copy.115
  71.3 7.2 reshape.558
  82.4 5.0 all_to_all.238
  91.3 5.4 reshape.551
  96.7 6.9 copy.144
  116.2 6.1 reshape.547
  122.3 6.9 copy.140
  142.1 6.1 reshape.559
  148.2 6.9 copy.146
  197.3 5.5 copy.141
  209.6 5.5 copy.147
  226.0 443.2 %while.16 = (s32[]{:T(128)}, bf16[64,32,160]{2,0,1:T(8,128)(2,1)}, f32[80,48,2,160]{3,1,2,0:T(8,128)}, s32[8]{0:T(128)S(1)}, s32[]{:T(128)}, /*index=5*/s32[32,4...) while((s32[]{:T(128)}, bf16[64,32,160]{2,0,1:T(8,128)(2,1)}, ...), condition=%wide.region_4.5_spmd, body=%wide.region_0.4_spmd.sunk | while | flops 243459376 | bytes 80320480 | solution.py:128
  247.7 4.6 fusion.69
  303.0 4.6 fusion.69
  358.3 4.6 fusion.69
  413.6 4.6 fusion.69
  468.9 4.6 fusion.69
  524.2 4.6 fusion.69
  676.4 7.1 copy.126
  683.5 5.4 all-to-all-start.8
  688.9 4.7 slice.201
  718.5 11.3 %all-to-all-done.9 = bf16[64,16,2,1,160]{4,1,3,2,0:T(8,128)(2,1)S(1)} async-done(((bf16[64,16,2,1,160]{4,1,3,2,0:T(8,128)(2,1)}), bf16[64,16,2,1,160]{4,1,3,2,0:T(8,128)(2,1)S(1)}, u32[]{:S(2)}, u32[]{:S(2)}) %all-to-all-start.9) | async-done | bytes 655392 | tf_op jit(solution)/shard_map/all_to_all | solution.py:189
  735.1 10.4 %all-to-all-done.13 = bf16[64,16,2,1,160]{4,1,3,2,0:T(8,128)(2,1)S(1)} async-done(((bf16[64,16,2,1,160]{4,1,3,2,0:T(8,128)(2,1)}), bf16[64,16,2,1,160]{4,1,3,2,0:T(8,128)(2,1)S(1)}, u32[]{:S(2)}, u32[]{:S(2)}) %all-to-all-start.13) | async-done | bytes 655392 | tf_op jit(solution)/shard_map/all_to_all | solution.py:203
  (511 shorter events, 563.7 us)
Async XLA Ops:
  6.4 12.1 %copy-start.3 = (bf16[16,16,1280]{2,1,0:T(8,128)(2,1)S(1)}, bf16[16,16,1280]{2,1,0:T(8,128)(2,1)}, u32[]{:S(2)}) copy-start(bf16[16,16,1280]{2,1,0:T(8,128)(2,1)} %param.12) | copy-start | bytes 1966084
  14.3 16.7 %all-to-all-start.2 = ((bf16[2,2,81920]{2,1,0:T(2,128)(2,1)}), bf16[2,2,81920]{2,1,0:T(2,128)(2,1)S(1)}, u32[]{:S(2)}, u32[]{:S(2)}) async-start(bf16[2,2,81920]{2,1,0:T(2,128)(2,1)} %reshape.554), calls=%async_computation.2 | async-start | bytes 1310720 | tf_op jit(solution)/shard_map/all_to_all | solution.py:152
  31.0 47.5 %all-to-all-start = ((bf16[2,2,81920]{2,1,0:T(2,128)(2,1)}), bf16[2,2,81920]{2,1,0:T(2,128)(2,1)}, u32[]{:S(2)}, u32[]{:S(2)}) async-start(bf16[2,2,81920]{2,1,0:T(2,128)(2,1)} %reshape.546), calls=%async_computation | async-start | bytes 1310720 | tf_op jit(solution)/shard_map/all_to_all | solution.py:145
  51.5 3.3 copy-start.4
  59.4 7.2 copy-start.5
  87.4 24.6 %all-to-all-start.3 = ((bf16[4,2,40960]{2,1,0:T(2,128)(2,1)}), bf16[4,2,40960]{2,1,0:T(2,128)(2,1)S(1)}, u32[]{:S(2)}, u32[]{:S(2)}) async-start(bf16[4,2,40960]{2,1,0:T(2,128)(2,1)} %reshape.556), calls=%async_computation.3 | async-start | bytes 1310720 | tf_op jit(solution)/shard_map/all_to_all | solution.py:151
  112.0 25.6 %all-to-all-start.5 = ((bf16[4,2,40960]{2,1,0:T(2,128)(2,1)}), bf16[4,2,40960]{2,1,0:T(2,128)(2,1)}, u32[]{:S(2)}, u32[]{:S(2)}) async-start(bf16[4,2,40960]{2,1,0:T(2,128)(2,1)} %reshape.552), calls=%async_computation.5 | async-start | bytes 1310720 | tf_op jit(solution)/shard_map/all_to_all | solution.py:158
  137.6 42.9 %all-to-all-start.1 = ((bf16[4,2,40960]{2,1,0:T(2,128)(2,1)}), bf16[4,2,40960]{2,1,0:T(2,128)(2,1)}, u32[]{:S(2)}, u32[]{:S(2)}) async-start(bf16[4,2,40960]{2,1,0:T(2,128)(2,1)} %reshape.548), calls=%async_computation.1 | async-start | bytes 1310720 | tf_op jit(solution)/shard_map/all_to_all | solution.py:144
  180.5 10.3 %copy-start.6 = (s32[32,4]{0,1:T(4,128)S(1)}, s32[32,4]{0,1:T(4,128)}, u32[]{:S(2)}) copy-start(s32[32,4]{0,1:T(4,128)} %param.16) | copy-start | bytes 1540
  180.5 24.7 %all-to-all-start.7 = ((bf16[4,2,40960]{2,1,0:T(2,128)(2,1)}), bf16[4,2,40960]{2,1,0:T(2,128)(2,1)}, u32[]{:S(2)}, u32[]{:S(2)}) async-start(bf16[4,2,40960]{2,1,0:T(2,128)(2,1)} %reshape.560), calls=%async_computation.7 | async-start | bytes 1310720 | tf_op jit(solution)/shard_map/all_to_all | solution.py:165
  185.5 32.0 %collective-permute-start = (bf16[8,48,2,160]{3,1,0,2:T(8,128)(2,1)}, bf16[8,48,2,160]{3,1,0,2:T(8,128)(2,1)}, u32[]{:S(2)}, u32[]{:S(2)}) collective-permute-start(bf16[8,48,2,160]{3,1,0,2:T(8,128)(2,1)} %get-tuple-element.243), channel_id=1, source_target_pairs={{0,8},{8,16},{16,24},{1,9},{9,17},{17,25},{2,10},{10,18},{18,26},{... | collective-permute-start | bytes 737288 | tf_op jit(solution)/shard_map/ppermute | solution.py:19
  188.7 28.8 %collective-permute-start.1 = (bf16[8,48,2,160]{3,1,0,2:T(8,128)(2,1)S(1)}, bf16[8,48,2,160]{3,1,0,2:T(8,128)(2,1)}, u32[]{:S(2)}, u32[]{:S(2)}) collective-permute-start(bf16[8,48,2,160]{3,1,0,2:T(8,128)(2,1)S(1)} %get-tuple-element.244), channel_id=1, source_target_pairs={{8,0},{16,8},{24,16},{9,1},{17,9},{25,17},{10,2},{18,10},{26,18},{... | collective-permute-start | bytes 737288 | tf_op jit(solution)/shard_map/ppermute | solution.py:20
  240.9 2.2 copy-start.1
  273.2 3.0 copy-start
  296.3 2.2 copy-start.1
  328.5 3.0 copy-start
  351.6 2.2 copy-start.1
  383.9 3.0 copy-start
  439.1 3.0 copy-start
  494.4 3.1 copy-start
  517.5 2.2 copy-start.1
  549.7 3.0 copy-start
  605.1 3.0 copy-start
  628.0 2.2 copy-start.1
  660.3 3.0 copy-start
  670.5 24.8 %collective-permute-start.2 = (f32[8,32,2,160]{3,1,0,2:T(8,128)S(1)}, f32[8,32,2,160]{3,1,0,2:T(8,128)S(1)}, u32[]{:S(2)}, u32[]{:S(2)}) collective-permute-start(f32[8,32,2,160]{3,1,0,2:T(8,128)S(1)} %get-tuple-element.242), channel_id=1, source_target_pairs={{0,8},{8,16},{16,24},{1,9},{9,17},{17,25},{2,10},{10,18},{18,26},{... | collective-permute-start | bytes 983048 | tf_op jit(solution)/shard_map/ppermute | solution.py:19
  674.5 22.7 %collective-permute-start.3 = (f32[8,32,2,160]{3,1,0,2:T(8,128)S(1)}, f32[8,32,2,160]{3,1,0,2:T(8,128)S(1)}, u32[]{:S(2)}, u32[]{:S(2)}) collective-permute-start(f32[8,32,2,160]{3,1,0,2:T(8,128)S(1)} %get-tuple-element.241), channel_id=1, source_target_pairs={{8,0},{16,8},{24,16},{9,1},{17,9},{25,17},{10,2},{18,10},{26,18},{... | collective-permute-start | bytes 983048 | tf_op jit(solution)/shard_map/ppermute | solution.py:20
  683.5 10.1 %all-to-all-start.8 = ((bf16[64,32,1,1,160]{4,0,3,2,1:T(8,128)(2,1)}), bf16[64,32,1,1,160]{4,0,3,2,1:T(8,128)(2,1)S(1)}, u32[]{:S(2)}, u32[]{:S(2)}) async-start(bf16[64,32,1,1,160]{4,0,3,2,1:T(8,128)(2,1)} %bitcast.46), calls=%async_computation.8 | async-start | bytes 2097152 | tf_op jit(solution)/shard_map/all_to_all | solution.py:190
  703.4 5.3 all-to-all-start.12
  713.3 16.5 %all-to-all-start.9 = ((bf16[64,16,2,1,160]{4,1,3,2,0:T(8,128)(2,1)}), bf16[64,16,2,1,160]{4,1,3,2,0:T(8,128)(2,1)S(1)}, u32[]{:S(2)}, u32[]{:S(2)}) async-start(bf16[64,16,2,1,160]{4,1,3,2,0:T(8,128)(2,1)} %bitcast.49), calls=%async_computation.9 | async-start | bytes 2097152 | tf_op jit(solution)/shard_map/all_to_all | solution.py:189
  729.7 15.8 %all-to-all-start.13 = ((bf16[64,16,2,1,160]{4,1,3,2,0:T(8,128)(2,1)}), bf16[64,16,2,1,160]{4,1,3,2,0:T(8,128)(2,1)S(1)}, u32[]{:S(2)}, u32[]{:S(2)}) async-start(bf16[64,16,2,1,160]{4,1,3,2,0:T(8,128)(2,1)} %bitcast.226), calls=%async_computation.13 | async-start | bytes 2097152 | tf_op jit(solution)/shard_map/all_to_all | solution.py:203
  745.5 16.5 %all-to-all-start.11 = ((bf16[64,16,2,1,160]{4,1,3,2,0:T(8,128)(2,1)}), bf16[64,16,2,1,160]{4,1,3,2,0:T(8,128)(2,1)S(1)}, u32[]{:S(2)}, u32[]{:S(2)}) async-start(bf16[64,16,2,1,160]{4,1,3,2,0:T(8,128)(2,1)} %bitcast.224), calls=%async_computation.11 | async-start | bytes 2097152 | tf_op jit(solution)/shard_map/all_to_all | solution.py:196
  (4 other events, 8.1 us)
where the time goes:
time: 779 us; the launch traced here: 765 us
  local copies, waits for them, and re-layouts  467 us (60%)
  other arithmetic  124 us (16%)
  matrix products  62.5 us (8%)
  starting transfers between devices  57.6 us (7%)
  waiting for transfers between devices  26.8 us (3%)
  blocking collectives  13.5 us (2%)
  loops' own time  12.6 us (2%)
    unnamed x31, local copies, waits for them, and re-layouts  100 us
    slice x32, local copies, waits for them, and re-layouts, tile_step(): totals = lax.dynamic_update_slice(totals, previous + kv_parts[b], place)  82.7 us
    dynamic_update_slice x24, other arithmetic, tile_step(): totals = lax.dynamic_update_slice(totals, previous + kv_parts[b], place)  70 us
    dot_general x40, matrix products, product(): return jnp.einsum(form, left, right, preferred_element_type=jnp.float32)  62.5 us
    squeeze x24, local copies, waits for them, and re-layouts, tile_step(): totals = lax.dynamic_update_slice(totals, previous + kv_parts[b], place)  59.9 us
    another operation x48, local copies, waits for them, and re-layouts, tile_step(): jnp.stack([key_band[:, b * tile_side:b * tile_side + col_count] for b in...  30.1 us
    slice x8, local copies, waits for them, and re-layouts, tile_step(): key_band[:, b * tile_side:b * tile_side + col_count]  24.1 us
    transpose x8, other arithmetic, tile_step(): kv_parts.transpose(4, 3, 5, 1, 6, 0, 2, 7)  19 us
  transfers between devices with their start and end apart: 15, of which 4 were waited for; matrix products, arithmetic and copies ran while one was open for 25% of the time, Pallas kernels for 0%

commit v1 on v0

v1 whole, which is shorter than its diff:
```python
import functools
import math

import jax
import jax.numpy as jnp
from jax import lax
from jax.experimental import pallas as pl
from jax.experimental.pallas import tpu as pltpu
from jax.sharding import PartitionSpec as P

HDIM = 80
TILE_SIDE = 8
LANES = 128
WINDOW = 256
MASKED = -1e30


def plan(half):
    cuts, steps = [0], []
    done_heads, done_lanes = 0, 0
    while cuts[-1] < half:
        stop = min(cuts[-1] + WINDOW, half)
        heads = stop // HDIM
        lanes = half if stop == half else heads * HDIM // LANES * LANES
        steps.append(((cuts[-1], stop - cuts[-1]), (done_heads, heads), (done_lanes, lanes - done_lanes)))
        cuts.append(stop)
        done_heads, done_lanes = heads, lanes
    return steps


def kernel(
    block_count_heads,
    block_count,
    q_ref, k_ref, v_ref, g_ref, pattern_ref, tissue_ref,
    dq_out, dk_out, dv_out,
    qx, gx, kx, vx, bias, key_acc, value_acc, stage, landed, dq_low, dk_low, dv_low,
    in_send, in_recv, own_sem, part_send, part_recv, out_send, out_recv, out_own,
):
    side = TILE_SIDE
    rows, cols, features = q_ref.shape
    half = features // 2
    wide = 2 * cols
    tile_rows, tile_cols = rows // side, wide // side
    near = (tile_rows + 1) * side
    me = lax.axis_index("cols")
    sib = 1 - me
    block = lax.axis_index("rows") * block_count_heads + lax.axis_index("heads")
    has_up, has_down = block > 0, block < block_count - 1

    def at_block(index, core):
        return {"rows": index // block_count_heads, "heads": index % block_count_heads, "cols": core}

    sibling = at_block(block, sib)
    beside = ((block - 1, has_up), (block + 1, has_down))
    mine = pl.ds(pl.multiple_of(me * cols, cols), cols)
    theirs = pl.ds(pl.multiple_of(sib * cols, cols), cols)

    def lanes_of(core, low, width):
        return pl.ds(pl.multiple_of(core * half + low, LANES), width)

    own = [
        pltpu.make_async_copy(src.at[:, :, lanes_of(me, 0, half)], dst, own_sem.at[i])
        for i, (src, dst) in enumerate(
            (
                (q_ref, qx.at[:, mine]),
                (k_ref, kx.at[pl.ds(side, rows), mine]),
                (v_ref, vx.at[pl.ds(side, rows), mine]),
                (g_ref, gx.at[:, mine]),
            )
        )
    ]
    for copy in own:
        copy.start()

    barrier = pltpu.get_barrier_semaphore()
    pl.semaphore_signal(barrier, inc=1, device_id=sibling, device_id_type=pl.DeviceIdType.MESH)
    for index, exists in beside:
        @pl.when(exists)
        def _():
            for core in range(2):
                pl.semaphore_signal(
                    barrier, inc=1, device_id=at_block(index, core), device_id_type=pl.DeviceIdType.MESH
                )
    pl.semaphore_wait(barrier, 1 + 2 * has_up.astype(jnp.int32) + 2 * has_down.astype(jnp.int32))

    def remote(src, dst, send, recv, device):
        return pltpu.make_async_remote_copy(
            src_ref=src, dst_ref=dst, send_sem=send, recv_sem=recv,
            device_id=device, device_id_type=pl.DeviceIdType.MESH,
        )

    steps = plan(half)
    source_rows = (pl.ds(0, side), pl.ds(rows - side, side))
    target_rows = (pl.ds(side + rows, side), pl.ds(0, side))

    def sibling_copies(step, columns):
        low, width = steps[step][0]
        pieces = (
            (q_ref, qx.at[:, columns, pl.ds(low, width)]),
            (k_ref, kx.at[pl.ds(side, rows), columns, pl.ds(low, width)]),
            (v_ref, vx.at[pl.ds(side, rows), columns, pl.ds(low, width)]),
            (g_ref, gx.at[:, columns, pl.ds(low, width)]),
        )
        return [
            remote(src.at[:, :, lanes_of(sib, low, width)], dst,
                   in_send.at[step, i], in_recv.at[step, i], sibling)
            for i, (src, dst) in enumerate(pieces)
        ]

    def halo_copy(step, way, which, target, from_core):
        low, width = steps[step][0]
        src, dst = ((k_ref, kx), (v_ref, vx))[which]
        first = 4 + way * 4 + which * 2
        columns = pl.ds(pl.multiple_of(from_core * cols, cols), cols)
        return remote(
            src.at[source_rows[way], :, lanes_of(target, low, width)],
            dst.at[target_rows[way], columns, pl.ds(low, width)],
            in_send.at[step, first + target], in_recv.at[step, first + from_core],
            at_block(beside[way][0], target),
        )

    for step in range(len(steps)):
        for way in range(2):
            @pl.when(beside[way][1])
            def _():
                for which in range(2):
                    for target in range(2):
                        halo_copy(step, way, which, target, me).start()
        for copy in sibling_copies(step, mine):
            copy.start()

    grid_rows = pattern_ref.shape[0]
    key_col = lax.broadcasted_iota(jnp.int32, (wide, side * wide), 0) // side
    query_col = lax.broadcasted_iota(jnp.int32, (wide, side * wide), 1) % wide // side
    for t in range(tile_rows):
        tile_row = block * tile_rows + t
        for a in range(3):
            key_row = tile_row + a - 1
            inside = ((key_row >= 0) & (key_row < grid_rows)).astype(jnp.int32)
            key_row = jnp.clip(key_row, 0, grid_rows - 1)
            entry = jnp.full((wide, side * wide), MASKED, jnp.float32)
            for at in range(tile_cols):
                bits = pattern_ref[tile_row, at]
                for b in range(3):
                    to = at + b - 1
                    if not 0 <= to < tile_cols:
                        continue
                    if a == 1 and b == 1:
                        value = jnp.float32(0.0)
                    else:
                        ok = ((bits >> (3 * a + b)) & 1) * tissue_ref[key_row, to] * inside
                        value = (1 - ok).astype(jnp.float32) * MASKED
                    entry = jnp.where((key_col == to) & (query_col == at), value, entry)
            bias[t, a] = entry

    key_acc[...] = jnp.zeros_like(key_acc)
    value_acc[...] = jnp.zeros_like(value_acc)
    dq_low[...] = jnp.zeros_like(dq_low)
    for way in range(2):
        @pl.when(jnp.logical_not(beside[1 - way][1]))
        def _():
            kx[target_rows[way]] = jnp.zeros((side, wide, half), kx.dtype)
            vx[target_rows[way]] = jnp.zeros((side, wide, half), vx.dtype)

    scale = 1.0 / math.sqrt(HDIM)
    to_power = scale * math.log2(math.e)
    queries_in, keys_in = side * wide, 3 * side * wide

    def dot(left, right, left_dim, right_dim):
        return lax.dot_general(
            left, right, (((left_dim,), (right_dim,)), ((), ())), preferred_element_type=jnp.float32
        )

    def one(t, head):
        tile = jnp.maximum((HDIM * head + HDIM - 1) // LANES - 1, 0)
        window = pl.ds(pl.multiple_of(tile * LANES, LANES), WINDOW)
        start = HDIM * head - tile * LANES
        lane = lax.broadcasted_iota(jnp.int32, (queries_in, WINDOW), 1)
        in_head = (lane >= start) & (lane < start + HDIM)
        q_rows, k_rows = pl.ds(t * side, side), pl.ds(t * side, 3 * side)
        raw_q = qx[q_rows, :, window].reshape(queries_in, WINDOW)
        raw_g = gx[q_rows, :, window].reshape(queries_in, WINDOW)
        query = jnp.where(in_head, raw_q, jnp.zeros_like(raw_q))
        grad = jnp.where(in_head, raw_g, jnp.zeros_like(raw_g))
        keys = kx[k_rows, :, window].reshape(keys_in, WINDOW)
        values = vx[k_rows, :, window].reshape(keys_in, WINDOW)
        scores = dot(keys, query, 1, 1).reshape(3, side, wide, queries_in) * to_power
        scores = (scores + bias[t][:, None]).reshape(keys_in, queries_in)
        weight_grad = dot(values, grad, 1, 1)
        powers = jnp.exp2(scores - jnp.max(scores, axis=0, keepdims=True))
        weights = powers * (1.0 / jnp.sum(powers, axis=0, keepdims=True))
        row_dot = jnp.sum(weights * weight_grad, axis=0, keepdims=True)
        score_grad = (weights * (weight_grad - row_dot)).astype(jnp.bfloat16)
        weights_low = weights.astype(jnp.bfloat16)
        key_part = dot(score_grad, query, 1, 0).reshape(3 * side, wide, WINDOW)
        value_part = dot(weights_low, grad, 1, 0).reshape(3 * side, wide, WINDOW)
        query_part = (dot(score_grad, keys, 0, 0) * scale).astype(jnp.bfloat16)
        key_acc[k_rows, :, window] += key_part
        value_acc[k_rows, :, window] += value_part
        old = dq_low[q_rows, :, window].reshape(queries_in, WINDOW)
        dq_low[q_rows, :, window] = jnp.where(in_head, query_part, old).reshape(side, wide, WINDOW)

    def part_copy(step, way, which):
        low, width = steps[step][2]
        place = (which, way, slice(None), slice(None), pl.ds(low, width))
        return remote(
            stage.at[place], landed.at[place],
            part_send.at[step, 2 * way + which], part_recv.at[step, 2 * way + which],
            at_block(beside[way][0], me),
        )

    outs = ((dq_low, dq_out), (dk_low, dk_out), (dv_low, dv_out))

    def out_copies(step, i):
        low, width = steps[step][2]
        src, dst = outs[i]
        kept = pltpu.make_async_copy(
            src.at[:, mine, pl.ds(low, width)], dst.at[:, :, lanes_of(me, low, width)], out_own.at[step, i]
        )
        sent = remote(
            src.at[:, theirs, pl.ds(low, width)], dst.at[:, :, lanes_of(me, low, width)],
            out_send.at[step, i], out_recv.at[step, i], sibling,
        )
        return kept, sent

    def out_arrival(step, i):
        low, width = steps[step][2]
        src, dst = outs[i]
        return remote(
            src.at[:, theirs, pl.ds(low, width)], dst.at[:, :, lanes_of(sib, low, width)],
            out_send.at[step, i], out_recv.at[step, i], sibling,
        )

    def finish(step):
        low, width = steps[step][2]
        lanes = pl.ds(low, width)
        for which, (acc, dst, factor) in enumerate(
            ((key_acc, dk_low, scale), (value_acc, dv_low, 1.0))
        ):
            for way in range(2):
                at = pl.ds((rows - side) if way == 0 else 0, side)
                at_acc = pl.ds(rows if way == 0 else side, side)
                total = acc[at_acc, :, lanes] * factor
                exists = beside[1 - way][1]

                @pl.when(exists)
                def _():
                    part_copy(step, way, which).wait_recv()
                    dst[at, :, lanes] = (
                        total + landed[which, way, :, :, lanes].astype(jnp.float32)
                    ).astype(dst.dtype)

                @pl.when(jnp.logical_not(exists))
                def _():
                    dst[at, :, lanes] = total.astype(dst.dtype)
            for copy in out_copies(step, 1 + which):
                copy.start()

    for step, (_, (first, stop), (low, width)) in enumerate(steps):
        if step == 0:
            for copy in own:
                copy.wait()
        for copy in sibling_copies(step, theirs):
            copy.wait_recv()
        for way in range(2):
            @pl.when(beside[1 - way][1])
            def _():
                for which in range(2):
                    for core in range(2):
                        halo_copy(step, way, which, core, core).wait_recv()

        def heads_step(head, carry):
            for t in range(tile_rows):
                one(t, head)
            return carry

        lax.fori_loop(first, stop, heads_step, 0)
        lanes = pl.ds(low, width)
        for way in range(2):
            edge = pl.ds(0 if way == 0 else side + rows, side)

            @pl.when(beside[way][1])
            def _():
                stage[0, way, :, :, lanes] = (key_acc[edge, :, lanes] * scale).astype(stage.dtype)
                part_copy(step, way, 0).start()
                stage[1, way, :, :, lanes] = value_acc[edge, :, lanes].astype(stage.dtype)
                part_copy(step, way, 1).start()
        for copy in out_copies(step, 0):
            copy.start()
        if step > 0:
            finish(step - 1)
    finish(len(steps) - 1)

    for step in range(len(steps)):
        for copy in sibling_copies(step, mine):
            copy.wait_send()
        for way in range(2):
            @pl.when(beside[way][1])
            def _():
                for which in range(2):
                    for target in range(2):
                        halo_copy(step, way, which, target, me).wait_send()
                    part_copy(step, way, which).wait_send()
        for i in range(3):
            kept, sent = out_copies(step, i)
            kept.wait()
            sent.wait_send()
            out_arrival(step, i).wait_recv()


def shards(block_count_heads, block_count, queries, key_rows, value_rows, out_grad, pattern, tissue):
    rows, cols, features = queries.shape
    half, wide, side = features // 2, 2 * cols, TILE_SIDE
    count = len(plan(half))
    low = jnp.bfloat16
    dma = pltpu.SemaphoreType.DMA
    full = jax.ShapeDtypeStruct((rows, cols, features), low)
    return pl.pallas_call(
        functools.partial(kernel, block_count_heads, block_count),
        out_shape=(full, full, full),
        in_specs=[pl.BlockSpec(memory_space=pl.ANY)] * 4 + [pl.BlockSpec(memory_space=pltpu.SMEM)] * 2,
        out_specs=[pl.BlockSpec(memory_space=pl.ANY)] * 3,
        scratch_shapes=[
            pltpu.VMEM((rows, wide, half), low),
            pltpu.VMEM((rows, wide, half), low),
            pltpu.VMEM((rows + 2 * side, wide, half), low),
            pltpu.VMEM((rows + 2 * side, wide, half), low),
            pltpu.VMEM((rows // side, 3, wide, side * wide), jnp.float32),
            pltpu.VMEM((rows + 2 * side, wide, half), jnp.float32),
            pltpu.VMEM((rows + 2 * side, wide, half), jnp.float32),
            pltpu.VMEM((2, 2, side, wide, half), low),
            pltpu.VMEM((2, 2, side, wide, half), low),
            pltpu.VMEM((rows, wide, half), low),
            pltpu.VMEM((rows, wide, half), low),
            pltpu.VMEM((rows, wide, half), low),
            dma((count, 12)),
            dma((count, 12)),
            dma((4,)),
            dma((count, 4)),
            dma((count, 4)),
            dma((count, 3)),
            dma((count, 3)),
            dma((count, 3)),
        ],
        compiler_params=pltpu.CompilerParams(
            collective_id=0, has_side_effects=True, vmem_limit_bytes=48 * 1024 * 1024
        ),
    )(queries, key_rows, value_rows, out_grad, pattern, tissue)


def solution(mesh):
    split = P(("rows", "heads"), "cols", None)
    heads = mesh.shape["heads"]
    return jax.shard_map(
        functools.partial(shards, heads, heads * mesh.shape["rows"]),
        mesh=mesh,
        in_specs=(split, split, split, split, P(), P()),
        out_specs=(split, split, split),
        check_vma=False,
    )
```

time: 779 us -> 80.4 us (0.10); the launches traced: 765 us -> 80.1 us
  local copies, waits for them, and re-layouts: 467 us -> 7.72 us
  other arithmetic: 124 us -> 0 us
  Pallas kernels: 0 us -> 71.7 us
  matrix products: 62.5 us -> 0 us
  starting transfers between devices: 57.6 us -> 0 us
  waiting for transfers between devices: 26.8 us -> 0 us
  blocking collectives: 13.5 us -> 0 us
  loops' own time: 12.6 us -> 0 us
    slice x51 -> x0, local copies, waits for them, and re-layouts: 118 us -> none  [the longest x32 82.7 us: tile_step(): totals = lax.dynamic_update_slice(totals, previous + kv_parts[b], place)]
    unnamed x31 -> x15, local copies, waits for them, and re-layouts: 100 us -> 7.72 us
    all_to_all x26 -> x0, local copies, waits for them, and re-layouts: 82.5 us -> none  [the longest x3 12 us: shards(): lax.all_to_all(value_rows, 'cols', split_axis=2, concat_axis=1, tiled=True)]
    pallas_call x0 -> x1, Pallas kernels: none -> 71.7 us  [shards(): pl.pallas_call(functools.partial(kernel, block_count_heads, block_count),...]
    dynamic_update_slice x24 -> x0, other arithmetic: 70 us -> none  [tile_step(): totals = lax.dynamic_update_slice(totals, previous + kv_parts[b], place)]
    dot_general x40 -> x0, matrix products: 62.5 us -> none  [product(): return jnp.einsum(form, left, right, preferred_element_type=jnp.float32)]
    squeeze x24 -> x0, local copies, waits for them, and re-layouts: 59.9 us -> none  [tile_step(): totals = lax.dynamic_update_slice(totals, previous + kv_parts[b], place)]
    all_to_all x11 -> x0, starting transfers between devices: 46.5 us -> none  [the longest x1 5.39 us: shards(): lax.all_to_all(query_five, 'cols', split_axis=1, concat_axis=2, tiled=True)]
  transfers between devices with their start and end apart: 15 -> 0, of which waited for: 4 -> 0; matrix products, arithmetic and copies ran while one was open for 25% -> 0% of each run, Pallas kernels for 0% -> 0%
where the time goes in v1:
time: 80.4 us; the launch traced here: 80.1 us
  Pallas kernels  71.7 us (89%)
  local copies, waits for them, and re-layouts  7.72 us (10%)
    pallas_call x1, Pallas kernels, shards(): pl.pallas_call(functools.partial(kernel, block_count_heads, block_count),...  71.7 us
    unnamed x15, local copies, waits for them, and re-layouts  7.72 us

profile of v1, /device:TPU:21, one launch (start us, length us, event | category | flops | bytes accessed | tf_op | source)
XLA Modules:
  0.0 80.1 jit_solution(16428737381858162563)
XLA Ops:
  0.6 0.0 copy-start.4
  0.6 0.8 copy.9.pattern_ref
  1.4 0.0 copy-done.4
  1.4 0.1 copy.10.tissue_ref
  1.5 0.0 copy-start
  1.5 1.1 %copy-done = bf16[16,16,1280]{2,1,0:T(8,128)(2,1)S(1)} copy-done((bf16[16,16,1280]{2,1,0:T(8,128)(2,1)S(1)}, bf16[16,16,1280]{2,1,0:T(8,128)(2,1)}, u32[]{:S(2)}) %copy-start) | copy-done | bytes 655384
  2.6 0.0 copy-start.1
  2.6 1.1 %copy-done.1 = bf16[16,16,1280]{2,1,0:T(8,128)(2,1)S(1)} copy-done((bf16[16,16,1280]{2,1,0:T(8,128)(2,1)S(1)}, bf16[16,16,1280]{2,1,0:T(8,128)(2,1)}, u32[]{:S(2)}) %copy-start.1) | copy-done | bytes 655384
  3.7 0.0 copy-start.2
  3.7 1.1 %copy-done.2 = bf16[16,16,1280]{2,1,0:T(8,128)(2,1)S(1)} copy-done((bf16[16,16,1280]{2,1,0:T(8,128)(2,1)S(1)}, bf16[16,16,1280]{2,1,0:T(8,128)(2,1)}, u32[]{:S(2)}) %copy-start.2) | copy-done | bytes 655384
  4.8 0.0 copy-start.3
  4.8 1.1 %copy-done.3 = bf16[16,16,1280]{2,1,0:T(8,128)(2,1)S(1)} copy-done((bf16[16,16,1280]{2,1,0:T(8,128)(2,1)S(1)}, bf16[16,16,1280]{2,1,0:T(8,128)(2,1)}, u32[]{:S(2)}) %copy-start.3) | copy-done | bytes 655384
  5.9 71.7 %shard_map.85 = (bf16[16,16,1280]{2,1,0:T(8,128)(2,1)S(1)}, bf16[16,16,1280]{2,1,0:T(8,128)(2,1)S(1)}, bf16[16,16,1280]{2,1,0:T(8,128)(2,1)S(1)}) custom-call(bf16[16,16,1280]{2,1,0:T(8,128)(2,1)S(1)} %copy-done, bf16[16,16,1280]{2,1,0:T(8,128)(2,1)S(1)} %copy-done.1, bf16[16,16,1280]{2,1,0:T(8,128)(2,1)S(1)} %copy-done.2, ...), custom_call_target="tpu_custom_call" | custom-call | tf_op jit(solution)/shard_map/pallas_call | solution.py:318
  77.5 0.8 %copy.14 = bf16[16,16,1280]{2,1,0:T(8,128)(2,1)} copy(bf16[16,16,1280]{2,1,0:T(8,128)(2,1)S(1)} %get-tuple-element.6) | data formatting | bytes 1310720
  78.4 0.8 %copy.15 = bf16[16,16,1280]{2,1,0:T(8,128)(2,1)} copy(bf16[16,16,1280]{2,1,0:T(8,128)(2,1)S(1)} %get-tuple-element.7) | data formatting | bytes 1310720
  79.2 0.8 %copy.16 = bf16[16,16,1280]{2,1,0:T(8,128)(2,1)} copy(bf16[16,16,1280]{2,1,0:T(8,128)(2,1)S(1)} %get-tuple-element.8) | data formatting | bytes 1310720
Async XLA Ops:
  0.6 0.8 copy-start.4
  1.5 1.1 %copy-start = (bf16[16,16,1280]{2,1,0:T(8,128)(2,1)S(1)}, bf16[16,16,1280]{2,1,0:T(8,128)(2,1)}, u32[]{:S(2)}) copy-start(bf16[16,16,1280]{2,1,0:T(8,128)(2,1)} %q_ref.1) | copy-start | bytes 1966084
  2.6 1.1 %copy-start.1 = (bf16[16,16,1280]{2,1,0:T(8,128)(2,1)S(1)}, bf16[16,16,1280]{2,1,0:T(8,128)(2,1)}, u32[]{:S(2)}) copy-start(bf16[16,16,1280]{2,1,0:T(8,128)(2,1)} %k_ref.1) | copy-start | bytes 1966084
  3.7 1.1 %copy-start.2 = (bf16[16,16,1280]{2,1,0:T(8,128)(2,1)S(1)}, bf16[16,16,1280]{2,1,0:T(8,128)(2,1)}, u32[]{:S(2)}) copy-start(bf16[16,16,1280]{2,1,0:T(8,128)(2,1)} %v_ref.1) | copy-start | bytes 1966084
  4.8 1.1 %copy-start.3 = (bf16[16,16,1280]{2,1,0:T(8,128)(2,1)S(1)}, bf16[16,16,1280]{2,1,0:T(8,128)(2,1)}, u32[]{:S(2)}) copy-start(bf16[16,16,1280]{2,1,0:T(8,128)(2,1)} %g_ref.1) | copy-start | bytes 1966084

commit v2 on v1

v2 whole, which is shorter than its diff:
```python
import functools
import math

import jax
import jax.numpy as jnp
from jax import lax
from jax.experimental import pallas as pl
from jax.experimental.pallas import tpu as pltpu
from jax.sharding import PartitionSpec as P

HDIM = 80
TILE_SIDE = 8
LANES = 128
WINDOW = 256
MASKED = -1e30


def plan(half):
    cuts, steps = [0], []
    done_heads, done_lanes = 0, 0
    while cuts[-1] < half:
        stop = min(cuts[-1] + WINDOW, half)
        heads = stop // HDIM
        lanes = half if stop == half else heads * HDIM // LANES * LANES
        steps.append(((cuts[-1], stop - cuts[-1]), (done_heads, heads), (done_lanes, lanes - done_lanes)))
        cuts.append(stop)
        done_heads, done_lanes = heads, lanes
    return steps


def kernel(
    block_count_heads,
    block_count,
    q_ref, k_ref, v_ref, g_ref, pattern_ref, tissue_ref,
    dq_out, dk_out, dv_out,
    qx, gx, kx, vx, bias, query_acc, key_acc, value_acc, stats, stats_in, stage, landed,
    dq_low, dk_low, dv_low,
    in_send, in_recv, own_sem, stat_send, stat_recv, part_send, part_recv, out_send, out_recv, out_own,
):
    side = TILE_SIDE
    rows, cols, features = q_ref.shape
    half = features // 2
    wide = 2 * cols
    tile_rows, tile_cols = rows // side, wide // side
    me = lax.axis_index("cols")
    sib = 1 - me
    block = lax.axis_index("rows") * block_count_heads + lax.axis_index("heads")
    has_up, has_down = block > 0, block < block_count - 1

    def at_block(index, core):
        return {"rows": index // block_count_heads, "heads": index % block_count_heads, "cols": core}

    sibling = at_block(block, sib)
    beside = ((block - 1, has_up), (block + 1, has_down))
    mine = pl.ds(pl.multiple_of(me * cols, cols), cols)
    theirs = pl.ds(pl.multiple_of(sib * cols, cols), cols)

    def lanes_of(core, low, width):
        return pl.ds(pl.multiple_of(core * half + low, LANES), width)

    own = [
        pltpu.make_async_copy(src.at[:, :, lanes_of(me, 0, half)], dst, own_sem.at[i])
        for i, (src, dst) in enumerate(
            (
                (q_ref, qx.at[pl.ds(side, rows), mine]),
                (k_ref, kx.at[:, mine]),
                (v_ref, vx.at[:, mine]),
                (g_ref, gx.at[pl.ds(side, rows), mine]),
            )
        )
    ]
    for copy in own:
        copy.start()

    barrier = pltpu.get_barrier_semaphore()
    pl.semaphore_signal(barrier, inc=1, device_id=sibling, device_id_type=pl.DeviceIdType.MESH)
    for index, exists in beside:
        @pl.when(exists)
        def _():
            for core in range(2):
                pl.semaphore_signal(
                    barrier, inc=1, device_id=at_block(index, core), device_id_type=pl.DeviceIdType.MESH
                )
    pl.semaphore_wait(barrier, 1 + 2 * has_up.astype(jnp.int32) + 2 * has_down.astype(jnp.int32))

    def remote(src, dst, send, recv, device):
        return pltpu.make_async_remote_copy(
            src_ref=src, dst_ref=dst, send_sem=send, recv_sem=recv,
            device_id=device, device_id_type=pl.DeviceIdType.MESH,
        )

    steps = plan(half)
    source_rows = (pl.ds(0, side), pl.ds(rows - side, side))
    target_rows = (pl.ds(side + rows, side), pl.ds(0, side))

    def sibling_copies(step, columns):
        low, width = steps[step][0]
        pieces = (
            (q_ref, qx.at[pl.ds(side, rows), columns, pl.ds(low, width)]),
            (k_ref, kx.at[:, columns, pl.ds(low, width)]),
            (v_ref, vx.at[:, columns, pl.ds(low, width)]),
            (g_ref, gx.at[pl.ds(side, rows), columns, pl.ds(low, width)]),
        )
        return [
            remote(src.at[:, :, lanes_of(sib, low, width)], dst,
                   in_send.at[step, i], in_recv.at[step, i], sibling)
            for i, (src, dst) in enumerate(pieces)
        ]

    def halo_copy(step, way, which, target, from_core):
        low, width = steps[step][0]
        src, dst = ((q_ref, qx), (g_ref, gx))[which]
        first = 4 + way * 4 + which * 2
        columns = pl.ds(pl.multiple_of(from_core * cols, cols), cols)
        return remote(
            src.at[source_rows[way], :, lanes_of(target, low, width)],
            dst.at[target_rows[way], columns, pl.ds(low, width)],
            in_send.at[step, first + target], in_recv.at[step, first + from_core],
            at_block(beside[way][0], target),
        )

    for step in range(len(steps)):
        for way in range(2):
            @pl.when(beside[way][1])
            def _():
                for which in range(2):
                    for target in range(2):
                        halo_copy(step, way, which, target, me).start()
        for copy in sibling_copies(step, mine):
            copy.start()

    query_rows = tile_rows + 2
    reach = [[at for at in (u - 2, u - 1, u) if 0 <= at < tile_rows] for u in range(query_rows)]
    first_mask = [sum(len(r) for r in reach[:u]) for u in range(query_rows)]
    grid_rows = pattern_ref.shape[0]
    key_col = lax.broadcasted_iota(jnp.int32, (wide, side * wide), 0) // side
    query_col = lax.broadcasted_iota(jnp.int32, (wide, side * wide), 1) % wide // side
    for u in range(query_rows):
        query_row = block * tile_rows + u - 1
        inside = ((query_row >= 0) & (query_row < grid_rows)).astype(jnp.int32)
        query_row = jnp.clip(query_row, 0, grid_rows - 1)
        for i, key_at in enumerate(reach[u]):
            a = key_at - u + 2
            key_row = block * tile_rows + key_at
            entry = jnp.full((wide, side * wide), MASKED, jnp.float32)
            for at in range(tile_cols):
                bits = pattern_ref[query_row, at]
                for b in range(3):
                    to = at + b - 1
                    if not 0 <= to < tile_cols:
                        continue
                    if a == 1 and b == 1:
                        value = jnp.float32(0.0)
                    else:
                        ok = ((bits >> (3 * a + b)) & 1) * tissue_ref[key_row, to] * inside
                        value = (1 - ok).astype(jnp.float32) * MASKED
                    entry = jnp.where((key_col == to) & (query_col == at), value, entry)
            bias[first_mask[u] + i] = entry

    key_acc[...] = jnp.zeros_like(key_acc)
    value_acc[...] = jnp.zeros_like(value_acc)
    query_acc[...] = jnp.zeros_like(query_acc)
    stats[...] = jnp.zeros_like(stats)
    for way in range(2):
        @pl.when(jnp.logical_not(beside[1 - way][1]))
        def _():
            qx[target_rows[way]] = jnp.zeros((side, wide, half), qx.dtype)
            gx[target_rows[way]] = jnp.zeros((side, wide, half), gx.dtype)
            for step in range(len(steps)):
                for i in range(2):
                    stats_in[2 - 2 * way + i, step] = jnp.full(stats_in.shape[2:], MASKED, jnp.float32)

    scale = 1.0 / math.sqrt(HDIM)
    to_power = scale * math.log2(math.e)
    queries_in = side * wide

    def dot(left, right, left_dim, right_dim):
        return lax.dot_general(
            left, right, (((left_dim,), (right_dim,)), ((), ())), preferred_element_type=jnp.float32
        )

    def prepare(head):
        tile = jnp.maximum((HDIM * head + HDIM - 1) // LANES - 1, 0)
        window = pl.ds(pl.multiple_of(tile * LANES, LANES), WINDOW)
        start = HDIM * head - tile * LANES
        lane = lax.broadcasted_iota(jnp.int32, (queries_in, WINDOW), 1)
        return window, (lane >= start) & (lane < start + HDIM)

    def pair(u, window, in_head):
        count = len(reach[u])
        keys_in = count * queries_in
        q_rows, k_rows = pl.ds(u * side, side), pl.ds(reach[u][0] * side, count * side)
        raw_q = qx[q_rows, :, window].reshape(queries_in, WINDOW)
        raw_g = gx[q_rows, :, window].reshape(queries_in, WINDOW)
        query = jnp.where(in_head, raw_q, jnp.zeros_like(raw_q))
        grad = jnp.where(in_head, raw_g, jnp.zeros_like(raw_g))
        keys = kx[k_rows, :, window].reshape(keys_in, WINDOW)
        values = vx[k_rows, :, window].reshape(keys_in, WINDOW)
        scores = dot(keys, query, 1, 1).reshape(count, side, wide, queries_in) * to_power
        masks = bias[first_mask[u] : first_mask[u] + count]
        scores = (scores + masks[:, None]).reshape(keys_in, queries_in)
        return q_rows, k_rows, query, grad, keys, scores, dot(values, grad, 1, 1)

    def measure(u, step, at, window, in_head):
        _, _, _, _, _, scores, weight_grad = pair(u, window, in_head)
        top = jnp.max(scores, axis=0, keepdims=True)
        powers = jnp.exp2(scores - top)
        total = jnp.sum(powers, axis=0, keepdims=True)
        part = jnp.sum(powers * weight_grad, axis=0, keepdims=True)
        stats[u, step, pl.ds(2 * at, 1), :] = top + jnp.log2(total)
        stats[u, step, pl.ds(2 * at + 1, 1), :] = part / total

    def gradients(u, step, at, window, in_head):
        q_rows, k_rows, query, grad, keys, scores, weight_grad = pair(u, window, in_head)
        here, there = stats[u, step, pl.ds(2 * at, 1), :], stats_in[u, step, pl.ds(2 * at, 1), :]
        top = jnp.maximum(here, there)
        power_here, power_there = jnp.exp2(here - top), jnp.exp2(there - top)
        total = power_here + power_there
        row_dot = (
            power_here * stats[u, step, pl.ds(2 * at + 1, 1), :]
            + power_there * stats_in[u, step, pl.ds(2 * at + 1, 1), :]
        ) / total
        weights = jnp.exp2(scores - top) * (1.0 / total)
        score_grad = (weights * (weight_grad - row_dot)).astype(jnp.bfloat16)
        weights_low = weights.astype(jnp.bfloat16)
        shape = (len(reach[u]) * side, wide, WINDOW)
        key_acc[k_rows, :, window] += dot(score_grad, query, 1, 0).reshape(shape)
        value_acc[k_rows, :, window] += dot(weights_low, grad, 1, 0).reshape(shape)
        query_part = dot(score_grad, keys, 0, 0) * scale
        old = query_acc[q_rows, :, window].reshape(queries_in, WINDOW)
        query_acc[q_rows, :, window] = jnp.where(in_head, query_part, old).reshape(side, wide, WINDOW)

    def each_head(step, act):
        first, stop = steps[step][1]

        def body(head, carry):
            window, in_head = prepare(head)
            for u in range(query_rows):
                act(u, step, head - first, window, in_head)
            return carry

        lax.fori_loop(first, stop, body, 0)

    def stat_copy(step, way):
        here, there = (0, query_rows - 2) if way == 0 else (query_rows - 2, 0)
        return remote(
            stats.at[pl.ds(here, 2), step], stats_in.at[pl.ds(there, 2), step],
            stat_send.at[step, way], stat_recv.at[step, way], at_block(beside[way][0], me),
        )

    def part_copy(step, way):
        low, width = steps[step][2]
        place = (way, slice(None), slice(None), pl.ds(low, width))
        return remote(
            stage.at[place], landed.at[place], part_send.at[step, way], part_recv.at[step, way],
            at_block(beside[way][0], me),
        )

    outs = ((dq_low, dq_out), (dk_low, dk_out), (dv_low, dv_out))

    def out_copies(step, i):
        low, width = steps[step][2]
        src, dst = outs[i]
        kept = pltpu.make_async_copy(
            src.at[:, mine, pl.ds(low, width)], dst.at[:, :, lanes_of(me, low, width)], out_own.at[step, i]
        )
        sent = remote(
            src.at[:, theirs, pl.ds(low, width)], dst.at[:, :, lanes_of(me, low, width)],
            out_send.at[step, i], out_recv.at[step, i], sibling,
        )
        return kept, sent

    def out_arrival(step, i):
        low, width = steps[step][2]
        src, dst = outs[i]
        return remote(
            src.at[:, theirs, pl.ds(low, width)], dst.at[:, :, lanes_of(sib, low, width)],
            out_send.at[step, i], out_recv.at[step, i], sibling,
        )

    def work(step):
        for way in range(2):
            @pl.when(beside[1 - way][1])
            def _():
                stat_copy(step, way).wait_recv()
        each_head(step, gradients)
        low, width = steps[step][2]
        lanes = pl.ds(low, width)
        for way in range(2):
            edge = pl.ds(0 if way == 0 else side + rows, side)

            @pl.when(beside[way][1])
            def _():
                stage[way, :, :, lanes] = query_acc[edge, :, lanes].astype(stage.dtype)
                part_copy(step, way).start()
        dk_low[:, :, lanes] = (key_acc[:, :, lanes] * scale).astype(dk_low.dtype)
        dv_low[:, :, lanes] = value_acc[:, :, lanes].astype(dv_low.dtype)
        for i in (1, 2):
            for copy in out_copies(step, i):
                copy.start()

    def finish(step):
        low, width = steps[step][2]
        lanes = pl.ds(low, width)
        for way in range(2):
            at = pl.ds((rows - side) if way == 0 else 0, side)
            total = query_acc[pl.ds(rows if way == 0 else side, side), :, lanes]
            exists = beside[1 - way][1]

            @pl.when(exists)
            def _():
                part_copy(step, way).wait_recv()
                dq_low[at, :, lanes] = (total + landed[way, :, :, lanes].astype(jnp.float32)).astype(dq_low.dtype)

            @pl.when(jnp.logical_not(exists))
            def _():
                dq_low[at, :, lanes] = total.astype(dq_low.dtype)
        for copy in out_copies(step, 0):
            copy.start()

    for step in range(len(steps)):
        if step == 0:
            for copy in own:
                copy.wait()
        for copy in sibling_copies(step, theirs):
            copy.wait_recv()
        for way in range(2):
            @pl.when(beside[1 - way][1])
            def _():
                for which in range(2):
                    for core in range(2):
                        halo_copy(step, way, which, core, core).wait_recv()
        each_head(step, measure)
        for way in range(2):
            @pl.when(beside[way][1])
            def _():
                stat_copy(step, way).start()
        if step > 0:
            work(step - 1)
        if step > 1:
            finish(step - 2)
    work(len(steps) - 1)
    for step in range(max(len(steps) - 2, 0), len(steps)):
        finish(step)

    for step in range(len(steps)):
        for copy in sibling_copies(step, mine):
            copy.wait_send()
        for way in range(2):
            @pl.when(beside[way][1])
            def _():
                for which in range(2):
                    for target in range(2):
                        halo_copy(step, way, which, target, me).wait_send()
                stat_copy(step, way).wait_send()
                part_copy(step, way).wait_send()
        for i in range(3):
            kept, sent = out_copies(step, i)
            kept.wait()
            sent.wait_send()
            out_arrival(step, i).wait_recv()


def shards(block_count_heads, block_count, queries, key_rows, value_rows, out_grad, pattern, tissue):
    rows, cols, features = queries.shape
    half, wide, side = features // 2, 2 * cols, TILE_SIDE
    count = len(plan(half))
    low = jnp.bfloat16
    dma = pltpu.SemaphoreType.DMA
    full = jax.ShapeDtypeStruct((rows, cols, features), low)
    return pl.pallas_call(
        functools.partial(kernel, block_count_heads, block_count),
        out_shape=(full, full, full),
        in_specs=[pl.BlockSpec(memory_space=pl.ANY)] * 4 + [pl.BlockSpec(memory_space=pltpu.SMEM)] * 2,
        out_specs=[pl.BlockSpec(memory_space=pl.ANY)] * 3,
        scratch_shapes=[
            pltpu.VMEM((rows + 2 * side, wide, half), low),
            pltpu.VMEM((rows + 2 * side, wide, half), low),
            pltpu.VMEM((rows, wide, half), low),
            pltpu.VMEM((rows, wide, half), low),
            pltpu.VMEM((3 * (rows // side), wide, side * wide), jnp.float32),
            pltpu.VMEM((rows + 2 * side, wide, half), jnp.float32),
            pltpu.VMEM((rows, wide, half), jnp.float32),
            pltpu.VMEM((rows, wide, half), jnp.float32),
            pltpu.VMEM((rows // side + 2, count, 8, side * wide), jnp.float32),
            pltpu.VMEM((rows // side + 2, count, 8, side * wide), jnp.float32),
            pltpu.VMEM((2, side, wide, half), low),
            pltpu.VMEM((2, side, wide, half), low),
            pltpu.VMEM((rows, wide, half), low),
            pltpu.VMEM((rows, wide, half), low),
            pltpu.VMEM((rows, wide, half), low),
            dma((count, 12)),
            dma((count, 12)),
            dma((4,)),
            dma((count, 2)),
            dma((count, 2)),
            dma((count, 2)),
            dma((count, 2)),
            dma((count, 3)),
            dma((count, 3)),
            dma((count, 3)),
        ],
        compiler_params=pltpu.CompilerParams(
            collective_id=0, has_side_effects=True, vmem_limit_bytes=60 * 1024 * 1024
        ),
    )(queries, key_rows, value_rows, out_grad, pattern, tissue)


def solution(mesh):
    split = P(("rows", "heads"), "cols", None)
    heads = mesh.shape["heads"]
    return jax.shard_map(
        functools.partial(shards, heads, heads * mesh.shape["rows"]),
        mesh=mesh,
        in_specs=(split, split, split, split, P(), P()),
        out_specs=(split, split, split),
        check_vma=False,
    )
```

time: 80.4 us -> 69.5 us (0.86)
  Pallas kernels: 71.7 us -> 62.2 us
  local copies, waits for them, and re-layouts: 7.72 us -> 6.26 us
    pallas_call x1, Pallas kernels: 71.7 us -> 62.2 us  [shards(): pl.pallas_call(functools.partial(kernel, block_count_heads, block_count),...]
    unnamed x15 -> x11, local copies, waits for them, and re-layouts: 7.72 us -> 6.26 us
where the time goes in v2:
time: 69.5 us; the launch traced here: 69.1 us
  Pallas kernels  62.2 us (89%)
  local copies, waits for them, and re-layouts  6.26 us (9%)
    pallas_call x1, Pallas kernels, shards(): pl.pallas_call(functools.partial(kernel, block_count_heads, block_count),...  62.2 us
    unnamed x11, local copies, waits for them, and re-layouts  6.26 us

profile of v2, /device:TPU:21, one launch (start us, length us, event | category | flops | bytes accessed | tf_op | source)
XLA Modules:
  0.0 69.1 jit_solution(8768649220331117851)
XLA Ops:
  0.6 0.0 copy-start.2
  0.6 1.4 %copy.9.pattern_ref = s32[32,4]{1,0:T(8,128)} copy(s32[32,4]{0,1:T(4,128)} %param.10) | data formatting | bytes 1024 | tf_op args[4]
  2.0 0.0 copy-done.2
  2.0 0.7 copy.10.tissue_ref
  2.7 62.2 %shard_map.85 = (bf16[16,16,1280]{2,1,0:T(8,128)(2,1)}, bf16[16,16,1280]{2,1,0:T(8,128)(2,1)}, bf16[16,16,1280]{2,1,0:T(8,128)(2,1)}) custom-call(bf16[16,16,1280]{2,1,0:T(8,128)(2,1)} %q_ref.1, bf16[16,16,1280]{2,1,0:T(8,128)(2,1)} %k_ref.1, bf16[16,16,1280]{2,1,0:T(8,128)(2,1)} %v_ref.1, bf16[16,16,1280]{2,1,0:T(8,128)(2,1)} %g_ref.1, ...), custom_call_target="tpu_custom_call" | custom-call | tf_op jit(solution)/shard_map/pallas_call | solution.py:371
  64.9 0.0 copy-start.1
  64.9 2.0 %copy.14 = bf16[16,16,1280]{2,1,0:T(8,128)(2,1)} copy(bf16[16,16,1280]{2,1,0:T(8,128)(2,1)} %get-tuple-element.6) | data formatting | bytes 1310720
  67.0 0.0 copy-done.1
  67.0 0.0 copy-start
  67.0 0.8 %copy.15 = bf16[16,16,1280]{2,1,0:T(8,128)(2,1)} copy(bf16[16,16,1280]{2,1,0:T(8,128)(2,1)S(1)} %copy-done.1) | data formatting | bytes 1310720
  67.8 0.5 copy-done
  68.3 0.8 %copy.16 = bf16[16,16,1280]{2,1,0:T(8,128)(2,1)} copy(bf16[16,16,1280]{2,1,0:T(8,128)(2,1)S(1)} %copy-done) | data formatting | bytes 1310720
Async XLA Ops:
  0.6 1.4 %copy-start.2 = (s32[32,4]{0,1:T(4,128)S(1)}, s32[32,4]{0,1:T(4,128)}, u32[]{:S(2)}) copy-start(s32[32,4]{0,1:T(4,128)} %param.11) | copy-start | bytes 1540
  64.9 2.0 %copy-start.1 = (bf16[16,16,1280]{2,1,0:T(8,128)(2,1)S(1)}, bf16[16,16,1280]{2,1,0:T(8,128)(2,1)}, u32[]{:S(2)}) copy-start(bf16[16,16,1280]{2,1,0:T(8,128)(2,1)} %get-tuple-element.7) | copy-start | bytes 1966084
  67.0 1.3 %copy-start = (bf16[16,16,1280]{2,1,0:T(8,128)(2,1)S(1)}, bf16[16,16,1280]{2,1,0:T(8,128)(2,1)}, u32[]{:S(2)}) copy-start(bf16[16,16,1280]{2,1,0:T(8,128)(2,1)} %get-tuple-element.8) | copy-start | bytes 1966084

commit v3 on v2

--- a/solution.py
+++ b/solution.py
@@ -16,25 +16,23 @@
 
 
 def plan(half):
-    cuts, steps = [0], []
-    done_heads, done_lanes = 0, 0
-    while cuts[-1] < half:
-        stop = min(cuts[-1] + WINDOW, half)
+    steps, arrived, done_heads, done_lanes = [], 0, 0, 0
+    while done_lanes < half:
+        stop = min(arrived + WINDOW, half)
         heads = stop // HDIM
-        lanes = half if stop == half else heads * HDIM // LANES * LANES
-        steps.append(((cuts[-1], stop - cuts[-1]), (done_heads, heads), (done_lanes, lanes - done_lanes)))
-        cuts.append(stop)
-        done_heads, done_lanes = heads, lanes
+        lanes = heads * HDIM // LANES * LANES
+        steps.append(((arrived, stop - arrived), (done_heads, heads), (done_lanes, lanes - done_lanes)))
+        arrived, done_heads, done_lanes = stop, heads, lanes
     return steps
 
 
 def kernel(
     block_count_heads,
     block_count,
-    q_ref, k_ref, v_ref, g_ref, pattern_ref, tissue_ref,
+    q_ref, k_ref, v_ref, g_ref, pattern_in, tissue_in,
     dq_out, dk_out, dv_out,
     qx, gx, kx, vx, bias, query_acc, key_acc, value_acc, stats, stats_in, stage, landed,
-    dq_low, dk_low, dv_low,
+    dq_low, dk_low, dv_low, pattern_ref, tissue_ref,
     in_send, in_recv, own_sem, stat_send, stat_recv, part_send, part_recv, out_send, out_recv, out_own,
 ):
     side = TILE_SIDE
@@ -69,7 +67,11 @@
             )
         )
     ]
-    for copy in own:
+    small = [
+        pltpu.make_async_copy(src, dst, own_sem.at[4 + i])
+        for i, (src, dst) in enumerate(((pattern_in, pattern_ref), (tissue_in, tissue_ref)))
+    ]
+    for copy in own + small:
         copy.start()
 
     barrier = pltpu.get_barrier_semaphore()
@@ -95,6 +97,8 @@
 
     def sibling_copies(step, columns):
         low, width = steps[step][0]
+        if not width:
+            return []
         pieces = (
             (q_ref, qx.at[pl.ds(side, rows), columns, pl.ds(low, width)]),
             (k_ref, kx.at[:, columns, pl.ds(low, width)]),
@@ -123,7 +127,7 @@
         for way in range(2):
             @pl.when(beside[way][1])
             def _():
-                for which in range(2):
+                for which in range(2 if steps[step][0][1] else 0):
                     for target in range(2):
                         halo_copy(step, way, which, target, me).start()
         for copy in sibling_copies(step, mine):
@@ -132,6 +136,8 @@
     query_rows = tile_rows + 2
     reach = [[at for at in (u - 2, u - 1, u) if 0 <= at < tile_rows] for u in range(query_rows)]
     first_mask = [sum(len(r) for r in reach[:u]) for u in range(query_rows)]
+    for copy in small:
+        copy.wait()
     grid_rows = pattern_ref.shape[0]
     key_col = lax.broadcasted_iota(jnp.int32, (wide, side * wide), 0) // side
     query_col = lax.broadcasted_iota(jnp.int32, (wide, side * wide), 1) % wide // side
@@ -239,7 +245,7 @@
                 act(u, step, head - first, window, in_head)
             return carry
 
-        lax.fori_loop(first, stop, body, 0)
+        lax.fori_loop(first, stop, body, 0, unroll=True)
 
     def stat_copy(step, way):
         here, there = (0, query_rows - 2) if way == 0 else (query_rows - 2, 0)
@@ -327,7 +333,7 @@
         for way in range(2):
             @pl.when(beside[1 - way][1])
             def _():
-                for which in range(2):
+                for which in range(2 if steps[step][0][1] else 0):
                     for core in range(2):
                         halo_copy(step, way, which, core, core).wait_recv()
         each_head(step, measure)
@@ -349,7 +355,7 @@
         for way in range(2):
             @pl.when(beside[way][1])
             def _():
-                for which in range(2):
+                for which in range(2 if steps[step][0][1] else 0):
                     for target in range(2):
                         halo_copy(step, way, which, target, me).wait_send()
                 stat_copy(step, way).wait_send()
@@ -371,7 +377,7 @@
     return pl.pallas_call(
         functools.partial(kernel, block_count_heads, block_count),
         out_shape=(full, full, full),
-        in_specs=[pl.BlockSpec(memory_space=pl.ANY)] * 4 + [pl.BlockSpec(memory_space=pltpu.SMEM)] * 2,
+        in_specs=[pl.BlockSpec(memory_space=pl.ANY)] * 6,
         out_specs=[pl.BlockSpec(memory_space=pl.ANY)] * 3,
         scratch_shapes=[
             pltpu.VMEM((rows + 2 * side, wide, half), low),
@@ -389,9 +395,11 @@
             pltpu.VMEM((rows, wide, half), low),
             pltpu.VMEM((rows, wide, half), low),
             pltpu.VMEM((rows, wide, half), low),
+            pltpu.SMEM(pattern.shape, pattern.dtype),
+            pltpu.SMEM(tissue.shape, tissue.dtype),
             dma((count, 12)),
             dma((count, 12)),
-            dma((4,)),
+            dma((6,)),
             dma((count, 2)),
             dma((count, 2)),
             dma((count, 2)),

time: 69.5 us -> 66.8 us (0.961)
  Pallas kernels: 62.2 us -> 59.7 us
    pallas_call x1, Pallas kernels: 62.2 us -> 59.7 us  [shards(): pl.pallas_call(functools.partial(kernel, block_count_heads, block_count),...]
where the time goes in v3:
time: 66.8 us; the launch traced here: 66.6 us
  Pallas kernels  59.7 us (89%)
  local copies, waits for them, and re-layouts  6.26 us (9%)
    pallas_call x1, Pallas kernels, shards(): pl.pallas_call(functools.partial(kernel, block_count_heads, block_count),...  59.7 us
    unnamed x11, local copies, waits for them, and re-layouts  6.26 us

profile of v3, /device:TPU:21, one launch (start us, length us, event | category | flops | bytes accessed | tf_op | source)
XLA Modules:
  0.0 66.6 jit_solution(16427650423761816052)
XLA Ops:
  0.6 0.0 copy-start.2
  0.6 1.4 %copy.9.pattern_in = s32[32,4]{1,0:T(8,128)} copy(s32[32,4]{0,1:T(4,128)} %param.10) | data formatting | bytes 1024 | tf_op args[4]
  2.0 0.0 copy-done.2
  2.0 0.7 %copy.10.tissue_in = s32[32,4]{1,0:T(8,128)} copy(s32[32,4]{0,1:T(4,128)S(1)} %copy-done.2) | data formatting | bytes 1024 | tf_op args[5]
  2.7 59.7 %shard_map.85 = (bf16[16,16,1280]{2,1,0:T(8,128)(2,1)}, bf16[16,16,1280]{2,1,0:T(8,128)(2,1)}, bf16[16,16,1280]{2,1,0:T(8,128)(2,1)}) custom-call(bf16[16,16,1280]{2,1,0:T(8,128)(2,1)} %q_ref.1, bf16[16,16,1280]{2,1,0:T(8,128)(2,1)} %k_ref.1, bf16[16,16,1280]{2,1,0:T(8,128)(2,1)} %v_ref.1, bf16[16,16,1280]{2,1,0:T(8,128)(2,1)} %g_ref.1, ...), custom_call_target="tpu_custom_call" | custom-call | tf_op jit(solution)/shard_map/pallas_call | solution.py:377
  62.4 0.0 copy-start.1
  62.4 2.0 %copy.14 = bf16[16,16,1280]{2,1,0:T(8,128)(2,1)} copy(bf16[16,16,1280]{2,1,0:T(8,128)(2,1)} %get-tuple-element.6) | data formatting | bytes 1310720
  64.4 0.0 copy-done.1
  64.4 0.0 copy-start
  64.4 0.8 %copy.15 = bf16[16,16,1280]{2,1,0:T(8,128)(2,1)} copy(bf16[16,16,1280]{2,1,0:T(8,128)(2,1)S(1)} %copy-done.1) | data formatting | bytes 1310720
  65.3 0.5 copy-done
  65.8 0.8 %copy.16 = bf16[16,16,1280]{2,1,0:T(8,128)(2,1)} copy(bf16[16,16,1280]{2,1,0:T(8,128)(2,1)S(1)} %copy-done) | data formatting | bytes 1310720
Async XLA Ops:
  0.6 1.4 %copy-start.2 = (s32[32,4]{0,1:T(4,128)S(1)}, s32[32,4]{0,1:T(4,128)}, u32[]{:S(2)}) copy-start(s32[32,4]{0,1:T(4,128)} %param.11) | copy-start | bytes 1540
  62.4 2.0 %copy-start.1 = (bf16[16,16,1280]{2,1,0:T(8,128)(2,1)S(1)}, bf16[16,16,1280]{2,1,0:T(8,128)(2,1)}, u32[]{:S(2)}) copy-start(bf16[16,16,1280]{2,1,0:T(8,128)(2,1)} %get-tuple-element.7) | copy-start | bytes 1966084
  64.4 1.3 %copy-start = (bf16[16,16,1280]{2,1,0:T(8,128)(2,1)S(1)}, bf16[16,16,1280]{2,1,0:T(8,128)(2,1)}, u32[]{:S(2)}) copy-start(bf16[16,16,1280]{2,1,0:T(8,128)(2,1)} %get-tuple-element.8) | copy-start | bytes 1966084
